TPU v7x, 32 devices: a whole 2x2x4 slice. The times are simulated.
32 devices in a mesh: gene: 4 (over z), cell: 2 (over y), site: 4 (over x, core).
Axes of the slice: x: 2, y: 2, z: 4, core: 2. Of those that a mesh axis runs over, the one named last changes fastest.
Arguments:
- expr: bfloat16 [1024, 20000], P('cell', 'gene'), may hold values from -6 to 6
- proj_weight: bfloat16 [20000, 512], P('gene'), may hold values from -0.0390625 to 0.0390625
- centroids: bfloat16 [8192, 512], P('site'), may hold values from -6 to 6
- growth: float32 [1024], P('cell'), may hold values from 0.5 to 6
- site_weight: float32 [8192], P('site'), may hold values from 0.5 to 6
Outputs:
- cell_pot: float32 [1024], P('cell')
- site_pot: float32 [8192], P('site')
- barycenter: float32 [8192, 512], P('site')
All inputs are finite; a program needn't handle non-finite values.
Results may differ from a plain program's by a relative error of at most 0.0033.
The roundings to bfloat16 on the way count: a program that leaves them out, or rounds other values in their place, can miss the bound.
Values may be sent and summed in bfloat16 or wider, within the bound.
A program may use at most 64 MiB of HBM per device.

v0:
```python
import jax
import jax.numpy as jnp
from jax import lax
from jax.sharding import PartitionSpec as P

ROUNDS = 2


EPSILON = 0.02


def merged(part, axis, combine):
    gathered = jax.tree.map(lambda a: lax.all_gather(a, axis), part)

    def take(source):
        return jax.tree.map(lambda a: lax.dynamic_index_in_dim(a, source, 0, False), gathered)

    return lax.fori_loop(
        1, lax.axis_size(axis), lambda source, state: combine(state, take(source)), take(0)
    )


def join_lse(first_pair, second_pair):
    peak = jnp.maximum(first_pair[0], second_pair[0])
    summed = first_pair[1] * jnp.exp(first_pair[0] - peak) + second_pair[1] * jnp.exp(
        second_pair[0] - peak
    )
    return (peak, summed)


def over_sites(scores):
    local_peak = jnp.max(scores, axis=1)
    local_sum = jnp.sum(jnp.exp(scores - local_peak[:, None]), axis=1)
    peak, summed = merged((local_peak, local_sum), "site", join_lse)
    return peak + jnp.log(summed)


def over_cells(scores):
    local_peak = jnp.max(scores, axis=0)
    local_sum = jnp.sum(jnp.exp(scores - local_peak[None, :]), axis=0)
    peak, summed = merged((local_peak, local_sum), "cell", join_lse)
    return peak + jnp.log(summed)


def shards(expr, proj_weight, centroids, growth, site_weight):
    cell_rows = expr.shape[0]
    features = proj_weight.shape[1]
    partial_term = jnp.dot(expr, proj_weight, preferred_element_type=jnp.float32)
    projected = lax.psum(partial_term, "gene").astype(jnp.bfloat16)
    proj_f = projected.astype(jnp.float32)
    cent_f = centroids.astype(jnp.float32)
    proj_norm = jnp.sum(proj_f * proj_f, axis=1) / features
    cent_norm = jnp.sum(cent_f * cent_f, axis=1) / features
    cross = lax.dot_general(
        projected, centroids, (((1,), (1,)), ((), ())), preferred_element_type=jnp.float32
    )
    distance = proj_norm[:, None] + cent_norm[None, :] - 2.0 * cross / features
    growth_total = lax.psum(jnp.sum(growth), "cell")
    weight_total = lax.psum(jnp.sum(site_weight), "site")
    log_a = jnp.log(growth / growth_total)
    site_share = site_weight / weight_total
    log_b = jnp.log(site_share)
    site_pot = jnp.zeros((centroids.shape[0],), jnp.float32)
    cell_pot = jnp.zeros((cell_rows,), jnp.float32)
    for turn in range(ROUNDS):
        cell_pot = EPSILON * log_a - EPSILON * over_sites((site_pot[None, :] - distance) / EPSILON)
        site_pot = EPSILON * log_b - EPSILON * over_cells((cell_pot[:, None] - distance) / EPSILON)
    coupling = jnp.exp((cell_pot[:, None] + site_pot[None, :] - distance) / EPSILON).astype(
        jnp.bfloat16
    )
    carried = lax.dot_general(
        coupling, projected, (((0,), (0,)), ((), ())), preferred_element_type=jnp.float32
    )
    summed = lax.psum(carried, "cell")
    barycenter = summed / site_share[:, None]
    return (cell_pot, site_pot, barycenter)


def solution(mesh):
    placed = (P("cell", "gene"), P("gene", None), P("site", None), P("cell"), P("site"))
    return jax.shard_map(
        shards,
        mesh=mesh,
        in_specs=placed,
        out_specs=(P("cell"), P("site"), P("site", None)),
        check_vma=False,
    )
```

profile of v0, /device:TPU:0, one launch (start us, length us, event | category | flops | bytes accessed | tf_op | source)
XLA Modules:
  0.0 255.8 jit_solution(6585582554413526351)
XLA Ops:
  7.2 0.0 all-reduce.3.cloned.1.call-start
  7.2 2.1 multiply_reduce_fusion
  9.3 0.0 copy-start.4
  9.3 8.0 %fusion.23 = f32[512,512]{1,0:T(8,128)} fusion(bf16[512,5000]{0,1:T(8,128)(2,1)} %param.9, bf16[5000,512]{1,0:T(8,128)(2,1)} %param.10), kind=kOutput, calls=%fused_computation.59 | convolution fusion | flops 2621440000 | bytes 11288576 | tf_op jit(solution)/shard_map/dot_general | solution.py:48
  17.3 45.8 %all-reduce.4 = bf16[512,512]{1,0:T(8,128)(2,1)S(1)} all-reduce(f32[512,512]{1,0:T(8,128)} %fusion.23), channel_id=1, replica_groups=mesh['gene'=4,'cell'=2,'site'=4] {'gene'}, use_global_device_ids=true, to_apply=%region_4.0 | all-reduce | flops 262144 | bytes 1572864 | tf_op jit(solution)/shard_map/psum | solution.py:49
  63.1 0.2 multiply_reduce_fusion.1
  63.3 0.0 copy-done.4
  63.3 1.6 fusion
  64.9 0.0 copy-start.7
  64.9 2.0 copy-done
  66.9 0.9 exponential_reduce_fusion.3
  67.8 5.2 %all-gather.9 = f32[4,1,512]{2,1,0:T(1,128)S(1)} all-gather(f32[1,1,512]{2,1,0:T(1,128)S(1)} %bitcast.52), channel_id=3, replica_groups=mesh['gene'=4,'cell'=2,'site'=4] {'site'}, dimensions={0}, use_global_device_ids=true | all-gather | bytes 10240 | tf_op jit(solution)/shard_map/all_gather | solution.py:13
  73.0 5.1 %all-gather.8 = f32[4,1,512]{2,1,0:T(1,128)S(1)} all-gather(f32[1,1,512]{2,1,0:T(1,128)S(1)} %bitcast.50), channel_id=2, replica_groups=mesh['gene'=4,'cell'=2,'site'=4] {'site'}, dimensions={0}, use_global_device_ids=true | all-gather | bytes 10240 | tf_op jit(solution)/shard_map/all_gather | solution.py:13
  78.1 0.0 copy-done.7
  78.2 0.6 reduce_sum.72
  78.8 5.5 %psum.28 = f32[]{:T(128)} all-reduce(f32[]{:T(128)} %reduce_sum.72), channel_id=1, replica_groups=mesh['gene'=4,'cell'=2,'site'=4] {'cell'}, use_global_device_ids=true, to_apply=%region_1.0 | all-reduce | flops 1 | bytes 8 | tf_op jit(solution)/shard_map/psum | solution.py:58
  84.3 0.1 while.22
  84.5 0.0 copy-start.1
  84.5 0.8 multiply_subtract_fusion.2
  85.3 0.0 copy-start.5
  85.3 3.1 %fusion.1 = f32[2048]{0:T(1024)S(1)} fusion(f32[512,2048]{1,0:T(8,128)} %copy-done, f32[512]{0:T(512)S(1)} %multiply_subtract_fusion.2), kind=kLoop, calls=%fused_computation.18 | loop fusion | flops 3143680 | bytes 4204544 | tf_op jit(solution)/shard_map/reduce_max | solution.py:39
  88.4 0.0 copy-done.1
  88.4 0.9 exponential_reduce_fusion.2
  89.3 4.4 %all-gather.2 = f32[4096]{0:T(1024)S(1)} all-gather(f32[2048]{0:T(1024)S(1)} %fusion.1), channel_id=4, replica_groups=mesh['gene'=4,'cell'=2,'site'=4] {'cell'}, dimensions={0}, use_global_device_ids=true | all-gather | bytes 24576 | tf_op jit(solution)/shard_map/all_gather | solution.py:13
  93.7 0.0 copy-done.5
  93.7 0.7 reduce_sum.73
  94.4 6.3 %psum.29 = f32[]{:T(128)} all-reduce(f32[]{:T(128)} %reduce_sum.73), channel_id=1, replica_groups=mesh['gene'=4,'cell'=2,'site'=4] {'site'}, use_global_device_ids=true, to_apply=%region_3.0 | all-reduce | flops 1 | bytes 8 | tf_op jit(solution)/shard_map/psum | solution.py:59
  100.7 4.5 %all-gather.3 = f32[4096]{0:T(1024)S(1)} all-gather(f32[2048]{0:T(1024)S(1)} %exponential_reduce_fusion.2), channel_id=5, replica_groups=mesh['gene'=4,'cell'=2,'site'=4] {'cell'}, dimensions={0}, use_global_device_ids=true | all-gather | bytes 24576 | tf_op jit(solution)/shard_map/all_gather | solution.py:13
  105.2 0.7 fusion.17
  105.9 2.7 %fusion.2 = f32[512]{0:T(512)S(1)} fusion(f32[512,2048]{1,0:T(8,128)} %copy-done, f32[2048]{0:T(1024)S(1)} %get-tuple-element.333), kind=kLoop, calls=%fused_computation.19 | loop fusion | flops 3145216 | bytes 4204544 | tf_op jit(solution)/shard_map/reduce_max | solution.py:32
  108.6 0.0 copy-done.2
  108.6 0.9 exponential_reduce_fusion.1
  109.5 5.2 %all-gather.10 = f32[4,1,512]{2,1,0:T(1,128)S(1)} all-gather(f32[1,1,512]{2,1,0:T(1,128)S(1)} %bitcast.49), channel_id=6, replica_groups=mesh['gene'=4,'cell'=2,'site'=4] {'site'}, dimensions={0}, use_global_device_ids=true | all-gather | bytes 10240 | tf_op jit(solution)/shard_map/all_gather | solution.py:13
  114.7 5.1 %all-gather.11 = f32[4,1,512]{2,1,0:T(1,128)S(1)} all-gather(f32[1,1,512]{2,1,0:T(1,128)S(1)} %bitcast.51), channel_id=7, replica_groups=mesh['gene'=4,'cell'=2,'site'=4] {'site'}, dimensions={0}, use_global_device_ids=true | all-gather | bytes 10240 | tf_op jit(solution)/shard_map/all_gather | solution.py:13
  119.9 0.1 while.23
  120.0 0.0 copy-start.3
  120.0 0.8 multiply_subtract_fusion.1
  120.8 0.0 copy-start.6
  120.8 2.9 %fusion.3 = f32[2048]{0:T(1024)S(1)} fusion(f32[512,2048]{1,0:T(8,128)} %copy-done, f32[512]{0:T(512)S(1)} %multiply_subtract_fusion.1), kind=kLoop, calls=%fused_computation.20 | loop fusion | flops 3143680 | bytes 4204544 | tf_op jit(solution)/shard_map/reduce_max | solution.py:39
  123.7 0.0 copy-done.3
  123.7 0.9 exponential_reduce_fusion
  124.6 4.4 %all-gather.6 = f32[4096]{0:T(1024)S(1)} all-gather(f32[2048]{0:T(1024)S(1)} %fusion.3), channel_id=8, replica_groups=mesh['gene'=4,'cell'=2,'site'=4] {'cell'}, dimensions={0}, use_global_device_ids=true | all-gather | bytes 24576 | tf_op jit(solution)/shard_map/all_gather | solution.py:13
  129.0 4.4 %all-gather.7 = f32[4096]{0:T(1024)S(1)} all-gather(f32[2048]{0:T(1024)S(1)} %exponential_reduce_fusion), channel_id=9, replica_groups=mesh['gene'=4,'cell'=2,'site'=4] {'cell'}, dimensions={0}, use_global_device_ids=true | all-gather | bytes 24576 | tf_op jit(solution)/shard_map/all_gather | solution.py:13
  133.4 0.0 copy-start.8
  133.4 3.5 %fusion.4 = f32[2048,512]{1,0:T(8,128)} fusion(f32[512,2048]{1,0:T(8,128)S(1)} %copy-done.3, f32[2048]{0:T(1024)S(1)} %fusion.12, f32[512]{0:T(512)S(1)} %multiply_subtract_fusion.1, bf16[512,512]{1,0:T(8,128)(2,1)S(1)} %all-reduce.4), kind=kOutput, calls=%fused_computation.21 | convolution fusion | flops 1077936128 | bytes 8923136 | tf_op jit(solution)/shard_map/dot_general | solution.py:71
  136.9 0.0 all-reduce.3.cloned.1.call-update
  136.9 107.5 %all-reduce.3.cloned.1.call-done = f32[2048,512]{1,0:T(8,128)} async-done(((f32[2048,512]{1,0:T(8,128)}), f32[2048,512]{1,0:T(8,128)}) %all-reduce.3.cloned.1.call-update) | async-done | bytes 4194320 | tf_op jit(solution)/shard_map/psum | solution.py:74
  244.4 4.5 %broadcast_divide_fusion = f32[2048,512]{1,0:T(8,128)} fusion(f32[2048,512]{1,0:T(8,128)} %all-reduce.3.cloned.1.call-done, f32[2048]{0:T(1024)S(1)} %get-tuple-element.334), kind=kLoop, calls=%fused_computation.22 | loop fusion | flops 1048576 | bytes 8396800 | tf_op jit(solution)/shard_map/div | solution.py:75
  (27 shorter events, 0.2 us)
Async XLA Ops:
  7.2 237.2 %all-reduce.3.cloned.1.call-start = ((), (), s32[]{:S(2)}) async-start(), calls=%async_computation | async-start | bytes 8388608 | tf_op jit(solution)/shard_map/psum | solution.py:74
  9.3 54.0 %copy-start.4 = (bf16[2048,512]{1,0:T(8,128)(2,1)S(1)}, bf16[2048,512]{1,0:T(8,128)(2,1)}, u32[]{:S(2)}) copy-start(bf16[2048,512]{1,0:T(8,128)(2,1)} %param.11) | copy-start | bytes 6291460
  64.9 2.0 copy-start
  64.9 13.3 %copy-start.7 = (f32[512]{0:T(512)S(1)}, f32[512]{0:T(512)}, u32[]{:S(2)}) copy-start(f32[512]{0:T(512)} %param.12) | copy-start | bytes 6148
  84.5 3.9 %copy-start.1 = (f32[512,2048]{1,0:T(8,128)S(1)}, f32[512,2048]{1,0:T(8,128)}, u32[]{:S(2)}) copy-start(f32[512,2048]{1,0:T(8,128)} %copy-done) | copy-start | bytes 12582916
  85.3 8.4 %copy-start.5 = (f32[2048]{0:T(1024)S(1)}, f32[2048]{0:T(1024)}, u32[]{:S(2)}) copy-start(f32[2048]{0:T(1024)} %param.13) | copy-start | bytes 24580
  100.7 7.9 %copy-start.2 = (f32[512,2048]{1,0:T(8,128)S(1)}, f32[512,2048]{1,0:T(8,128)}, u32[]{:S(2)}) copy-start(f32[512,2048]{1,0:T(8,128)} %copy-done) | copy-start | bytes 12582916
  120.0 3.7 %copy-start.3 = (f32[512,2048]{1,0:T(8,128)S(1)}, f32[512,2048]{1,0:T(8,128)}, u32[]{:S(2)}) copy-start(f32[512,2048]{1,0:T(8,128)} %copy-done) | copy-start | bytes 12582916
  120.8 12.5 %copy-start.6 = (f32[512]{0:T(512)}, f32[512]{0:T(512)S(1)}, u32[]{:S(2)}) copy-start(f32[512]{0:T(512)S(1)} %multiply_subtract_fusion.1) | copy-start | bytes 6148
  133.4 3.5 %copy-start.8 = (f32[2048]{0:T(1024)}, f32[2048]{0:T(1024)S(1)}, u32[]{:S(2)}) copy-start(f32[2048]{0:T(1024)S(1)} %fusion.12) | copy-start | bytes 24580
Sparse Core Ops, SparseCore 0:
  137.1 107.3 all-reduce.2
where the time goes:
time: 256 us
  waiting for transfers between devices  107 us (42%)
  blocking collectives  95.9 us (37%)
  other arithmetic  22.9 us (9%)
  between operations  14.2 us (6%)
  matrix products  13.1 us (5%)
    psum x1, waiting for transfers between devices, shards(): summed = lax.psum(carried, 'cell')  107 us
    psum x1, blocking collectives, shards(): projected = lax.psum(partial_term, 'gene').astype(jnp.bfloat16)  45.8 us
    all_gather x8, blocking collectives, merged(): gathered = jax.tree.map(lambda a: lax.all_gather(a, axis), part)  38.2 us
    dot_general x1, matrix products, shards(): jnp.dot(expr, proj_weight, preferred_element_type=jnp.float32)  8 us
    psum x1, blocking collectives, shards(): weight_total = lax.psum(jnp.sum(site_weight), 'site')  6.35 us
    reduce_max x2, other arithmetic, over_cells(): local_peak = jnp.max(scores, axis=0)  5.95 us
    psum x1, blocking collectives, shards(): growth_total = lax.psum(jnp.sum(growth), 'cell')  5.55 us
  transfers between devices with their start and end apart: 1, of which 1 were waited for; matrix products, arithmetic and copies ran while one was open for 0% of the time, Pallas kernels for 0%

commit v1 on v0

--- a/solution.py
+++ b/solution.py
@@ -1,6 +1,11 @@
+import functools
+import math
+
 import jax
 import jax.numpy as jnp
 from jax import lax
+from jax.experimental import pallas as pl
+from jax.experimental.pallas import tpu as pltpu
 from jax.sharding import PartitionSpec as P
 
 ROUNDS = 2
@@ -76,10 +81,358 @@
     return (cell_pot, site_pot, barycenter)
 
 
+MESH = pl.DeviceIdType.MESH
+LOG2E = 1.0 / math.log(2.0)
+LN2 = math.log(2.0)
+GENE, CELL, SITE = 4, 2, 4
+LANES = 128
+TALL = 256
+
+
+def tiled(column, width):
+    return jnp.concatenate([column] * (width // LANES), axis=1)
+
+
+def diagonal():
+    rows = lax.broadcasted_iota(jnp.int32, (LANES, LANES), 0)
+    return rows == lax.broadcasted_iota(jnp.int32, (LANES, LANES), 1)
+
+
+def to_column(row):
+    spread = jnp.where(diagonal(), jnp.broadcast_to(row, (LANES, LANES)), 0.0)
+    return jnp.broadcast_to(jnp.sum(spread, axis=1, keepdims=True), (LANES, LANES))
+
+
+def to_row(column):
+    return jnp.sum(jnp.where(diagonal(), column, 0.0), axis=0, keepdims=True)
+
+
+def scaled_norms(block, scale):
+    block = block.astype(jnp.float32)
+    total = jnp.sum(block * block, axis=1, keepdims=True) * scale
+    return jnp.broadcast_to(total, (block.shape[0], LANES))
+
+
+def fold(scores_ref, pot, start, lane, state):
+    peak, total = state
+    block = scores_ref[pl.ds(start, TALL), lane * LANES : (lane + 1) * LANES]
+    block = (block + pot).reshape(TALL // 8, 8, LANES)
+    new_peak = jnp.maximum(peak, jnp.max(block, axis=0))
+    total = total * jnp.exp2(peak - new_peak) + jnp.sum(jnp.exp2(block - new_peak[None]), axis=0)
+    return new_peak, total
+
+
+def close(state):
+    peak, total = state
+    top = jnp.max(peak, axis=0, keepdims=True)
+    return top, jnp.sum(total * jnp.exp2(peak - top), axis=0, keepdims=True)
+
+
+def prepare_kernel(
+    part_ref, cent_hbm, growth_ref, weight_ref,
+    proj_out, pot_out, cell_out, weight_out,
+    cent, arrived, proj, scores, site_pot, log_share, grow, message,
+    local_sem, reduce_send, reduce_recv, z_send, z_recv, x_send, x_recv, y_send, y_recv,
+    diag_send, diag_recv, core_send, core_recv, grow_send, grow_recv, lse_send, lse_recv,
+):
+    gene, cell, site = lax.axis_index("gene"), lax.axis_index("cell"), lax.axis_index("site")
+    cell_rows = growth_ref.shape[1]
+    cells = CELL * cell_rows
+    sites, features = cent.shape
+    strip = cell_rows // SITE
+    piece = strip // GENE
+    other_cell = 1 - cell
+    x_site = lax.rem(site + 2, SITE)
+    core_site = site + 1 - 2 * lax.rem(site, 2)
+    far_site = lax.rem(core_site + 2, SITE)
+    genes = [gene] + [lax.rem(gene + d, GENE) for d in range(1, GENE)]
+    back = [gene] + [lax.rem(gene + GENE - d, GENE) for d in range(1, GENE)]
+    peers = [(genes[d], cell, site) for d in range(1, GENE)]
+    x_dev, y_dev = (gene, cell, x_site), (gene, other_cell, site)
+    core_dev, far_dev = (gene, cell, core_site), (gene, cell, far_site)
+    site_devs = [(core_dev, core_site), (x_dev, x_site), (far_dev, far_site)]
+
+    def remote(src, dst, send, recv, device):
+        return pltpu.make_async_remote_copy(
+            src_ref=src, dst_ref=dst, send_sem=send, recv_sem=recv,
+            device_id=device, device_id_type=MESH,
+        )
+
+    load = pltpu.make_async_copy(cent_hbm, cent, local_sem)
+    load.start()
+    barrier = pltpu.get_barrier_semaphore()
+    everyone = peers + [x_dev, y_dev, core_dev, far_dev]
+    for device in everyone:
+        pl.semaphore_signal(barrier, inc=1, device_id=device, device_id_type=MESH)
+    pl.semaphore_wait(barrier, len(everyone))
+
+    sent = []
+
+    reduce = []
+    for d in range(1, GENE):
+        copy = remote(
+            part_ref.at[pl.ds(pl.multiple_of(genes[d] * piece, piece), piece)],
+            arrived.at[d - 1], reduce_send.at[d - 1], reduce_recv.at[d - 1], peers[d - 1],
+        )
+        copy.start()
+        reduce.append(copy)
+    grow[cell] = growth_ref[...]
+    growth_copy = remote(grow.at[cell], grow.at[cell], grow_send, grow_recv, y_dev)
+    growth_copy.start()
+
+    norm_scale = LOG2E / (features * EPSILON)
+    weight = weight_ref[...]
+    load.wait()
+
+    def norms(step, carry):
+        start = pl.multiple_of(step * LANES, LANES)
+        site_pot[pl.ds(start, LANES), :] = -scaled_norms(cent[pl.ds(start, LANES), :], norm_scale)
+        log_share[pl.ds(start, LANES), :] = to_column(weight_ref[pl.ds(step, 1), :])
+        return carry
+
+    lax.fori_loop(0, sites // LANES, norms, 0)
+    weight_sum = jnp.sum(jnp.sum(weight, axis=0, keepdims=True), axis=1, keepdims=True)
+    weight_row = jnp.broadcast_to(weight_sum, (1, LANES))
+
+    def rows(cell_at, site_at, gene_at):
+        at = cell_at * cell_rows + site_at * strip + gene_at * piece
+        return proj.at[pl.ds(pl.multiple_of(at, piece), piece)]
+
+    def group(cell_at, site_at):
+        at = cell_at * cell_rows + site_at * strip
+        return proj.at[pl.ds(pl.multiple_of(at, strip), strip)]
+
+    def send(ref, send_sem, recv_sem, device):
+        copy = remote(ref, ref, send_sem, recv_sem, device)
+        copy.start()
+        sent.append(copy)
+
+    def await_piece(ref, send_sem, recv_sem, device):
+        remote(ref, ref, send_sem, recv_sem, device).wait_recv()
+
+    total = part_ref[pl.ds(pl.multiple_of(gene * piece, piece), piece), :]
+    for d in range(1, GENE):
+        reduce[d - 1].wait_recv()
+        total = total + arrived[d - 1]
+    own_at = cell * cell_rows + site * strip + gene * piece
+    proj[pl.ds(pl.multiple_of(own_at, piece), piece), :] = total.astype(jnp.bfloat16)
+
+    for d in range(1, GENE):
+        send(rows(cell, site, gene), z_send.at[d - 1], z_recv.at[d - 1], peers[d - 1])
+    for d in range(GENE):
+        block = rows(cell, site, back[d])
+        if d > 0:
+            await_piece(block, z_send.at[d - 1], z_recv.at[d - 1], peers[d - 1])
+        send(block, x_send.at[d], x_recv.at[d], x_dev)
+        send(block, y_send.at[d], y_recv.at[d], y_dev)
+    send(group(cell, site), core_send.at[0], core_recv.at[0], core_dev)
+    for d in range(GENE):
+        block = rows(cell, x_site, back[d])
+        await_piece(block, x_send.at[d], x_recv.at[d], x_dev)
+        if d < 2:
+            send(block, diag_send.at[d], diag_recv.at[d], y_dev)
+        block = rows(other_cell, site, back[d])
+        await_piece(block, y_send.at[d], y_recv.at[d], y_dev)
+        if d >= 2:
+            send(block, diag_send.at[d], diag_recv.at[d], x_dev)
+    send(group(cell, x_site), core_send.at[1], core_recv.at[1], core_dev)
+    send(group(other_cell, site), core_send.at[2], core_recv.at[2], core_dev)
+    for d in range(GENE):
+        await_piece(
+            rows(other_cell, x_site, back[d]), diag_send.at[d], diag_recv.at[d],
+            y_dev if d < 2 else x_dev,
+        )
+    send(group(other_cell, x_site), core_send.at[3], core_recv.at[3], core_dev)
+    for at, (cell_at, site_at) in enumerate(
+        ((cell, core_site), (cell, far_site), (other_cell, core_site), (other_cell, far_site))
+    ):
+        await_piece(group(cell_at, site_at), core_send.at[at], core_recv.at[at], core_dev)
+
+    scale = 2.0 * norm_scale
+    blocks = cells // LANES
+    start_state = (
+        jnp.full((8, LANES), -1e38, jnp.float32), jnp.zeros((8, LANES), jnp.float32)
+    )
+
+    def first(step, states):
+        start = pl.multiple_of(step * TALL, TALL)
+        scores[pl.ds(start, TALL), :] = scale * lax.dot_general(
+            cent[pl.ds(start, TALL), :], proj[...], (((1,), (1,)), ((), ())),
+            preferred_element_type=jnp.float32,
+        )
+        pot = site_pot[pl.ds(start, TALL), :]
+        return tuple(fold(scores, pot, start, lane, states[lane]) for lane in range(blocks))
+
+    states = lax.fori_loop(0, sites // TALL, first, (start_state,) * blocks)
+
+    def exchange(turn, states):
+        closed = [close(state) for state in states]
+        peak = jnp.concatenate([pair[0] for pair in closed], axis=1)
+        summed = jnp.concatenate([pair[1] for pair in closed], axis=1)
+        message[turn, site] = jnp.concatenate([peak, summed, weight_row], axis=1)
+        for at, (device, _) in enumerate(site_devs):
+            own = message.at[turn, site]
+            send(own, lse_send.at[turn, at], lse_recv.at[turn, at], device)
+        for at, (device, source) in enumerate(site_devs):
+            slot = message.at[turn, source]
+            await_piece(slot, lse_send.at[turn, at], lse_recv.at[turn, at], device)
+        parts = [message[turn, s] for s in range(SITE)]
+        peak = functools.reduce(jnp.maximum, [part[:, :cells] for part in parts])
+        summed = sum(part[:, cells : 2 * cells] * jnp.exp2(part[:, :cells] - peak) for part in parts)
+        weight_total = sum(part[:, 2 * cells :] for part in parts)
+        return peak + jnp.log(summed) * LOG2E, weight_total
+
+    lse, weight_total = exchange(0, states)
+    growth_copy.wait_send()
+    slot = grow.at[other_cell]
+    await_piece(slot, grow_send, grow_recv, y_dev)
+    growth = jnp.concatenate([grow[c] for c in range(CELL)], axis=1)
+    log_a = jnp.log(growth / jnp.sum(growth, axis=1, keepdims=True)) * LOG2E
+    pot = log_a - lse
+
+    rows_at_once = 32
+
+    def second(step, states):
+        start = pl.multiple_of(step * TALL, TALL)
+        for sub in range(TALL // rows_at_once):
+            at = pl.ds(start + sub * rows_at_once, rows_at_once)
+            block = scores[at, :] + pot
+            peak = jnp.max(block, axis=1, keepdims=True)
+            summed = jnp.sum(jnp.exp2(block - peak), axis=1, keepdims=True)
+            share = log_share[at, :] / weight_total
+            site_pot[at, :] = jnp.log(share / summed) * LOG2E - peak
+        new = site_pot[pl.ds(start, TALL), :]
+        return tuple(fold(scores, new, start, lane, states[lane]) for lane in range(blocks))
+
+    states = lax.fori_loop(0, sites // TALL, second, (start_state,) * blocks)
+    lse, _ = exchange(1, states)
+    pot = log_a - lse
+
+    proj_out[...] = proj[...]
+    pot_out[...] = pot
+    weight_out[...] = weight_total
+    own = proj[pl.ds(pl.multiple_of(cell * cell_rows, cell_rows), cell_rows), :].astype(jnp.float32)
+    square = own * own
+    high = square.astype(jnp.bfloat16)
+    low = (square - high.astype(jnp.float32)).astype(jnp.bfloat16)
+    ones = jnp.ones((16, features), jnp.bfloat16)
+    norm = sum(
+        lax.dot_general(ones, half, (((1,), (1,)), ((), ())), preferred_element_type=jnp.float32)
+        for half in (high, low)
+    )[:1]
+    own_pot = jnp.where(cell == 0, pot[:, :cell_rows], pot[:, cell_rows:])
+    cell_out[...] = (EPSILON * LN2) * own_pot + norm * (1.0 / features)
+    for copy in sent:
+        copy.wait_send()
+    for copy in reduce:
+        copy.wait_send()
+
+
+def transport_kernel(
+    cent_ref, proj_ref, pot_ref, cell_ref, weight_ref, total_ref, cell_out, site_out, bary_out
+):
+    features = cent_ref.shape[1]
+    norm_scale = LOG2E / (features * EPSILON)
+    cell_out[...] = cell_ref[...]
+    pot = pot_ref[...]
+    weight_total = total_ref[...]
+    count = cent_ref.shape[0] // LANES
+    for sub in range(count):
+        at = pl.ds(sub * LANES, LANES)
+        cent = cent_ref[at, :]
+        block = (2.0 * norm_scale) * lax.dot_general(
+            cent, proj_ref[...], (((1,), (1,)), ((), ())), preferred_element_type=jnp.float32
+        )
+        block = block + pot
+        peak = jnp.max(block, axis=1, keepdims=True)
+        block = jnp.exp2(block - peak)
+        summed = jnp.sum(block, axis=1, keepdims=True)
+        share = to_column(weight_ref[0, sub : sub + 1, :]) / weight_total
+        ratio = share / summed
+        site_pot = (EPSILON * LN2) * (jnp.log(ratio) * LOG2E - peak) + scaled_norms(
+            cent, 1.0 / features
+        )
+        site_out[0, sub : sub + 1, :] = to_row(site_pot)
+        coupling = (block * tiled(ratio, block.shape[1])).astype(jnp.bfloat16)
+        carried = jnp.dot(coupling, proj_ref[...], preferred_element_type=jnp.float32)
+        bary_out[at, :] = carried * tiled(1.0 / share, features)
+
+
+def fused_shards(expr, proj_weight, centroids, growth, site_weight):
+    cell_rows, genes = expr.shape
+    sites, features = centroids.shape
+    strip = cell_rows // SITE
+    cells = CELL * cell_rows
+    quarter = lax.dynamic_slice(expr, (lax.axis_index("site") * strip, 0), (strip, genes))
+    part = jnp.dot(quarter, proj_weight, preferred_element_type=jnp.float32)
+    vmem = pl.BlockSpec(memory_space=pltpu.VMEM)
+    weight = site_weight.reshape(sites // LANES, LANES)
+    dma = pltpu.SemaphoreType.DMA
+    proj, pot, cell_pot, total = pl.pallas_call(
+        prepare_kernel,
+        out_shape=(
+            jax.ShapeDtypeStruct((cells, features), jnp.bfloat16),
+            jax.ShapeDtypeStruct((1, cells), jnp.float32),
+            jax.ShapeDtypeStruct((1, cell_rows), jnp.float32),
+            jax.ShapeDtypeStruct((1, LANES), jnp.float32),
+        ),
+        in_specs=[vmem, pl.BlockSpec(memory_space=pl.ANY), vmem, vmem],
+        out_specs=(vmem,) * 4,
+        scratch_shapes=[
+            pltpu.VMEM((sites, features), jnp.bfloat16),
+            pltpu.VMEM((GENE - 1, strip // GENE, features), jnp.float32),
+            pltpu.VMEM((cells, features), jnp.bfloat16),
+            pltpu.VMEM((sites, cells), jnp.float32),
+            pltpu.VMEM((sites, LANES), jnp.float32),
+            pltpu.VMEM((sites, LANES), jnp.float32),
+            pltpu.VMEM((CELL, 1, cell_rows), jnp.float32),
+            pltpu.VMEM((ROUNDS, SITE, 1, 2 * cells + LANES), jnp.float32),
+            dma, dma((3,)), dma((3,)), dma((3,)), dma((3,)),
+            dma((4,)), dma((4,)), dma((4,)), dma((4,)), dma((4,)), dma((4,)), dma((4,)), dma((4,)),
+            dma, dma, dma((ROUNDS, 3)), dma((ROUNDS, 3)),
+        ],
+        compiler_params=pltpu.CompilerParams(
+            collective_id=0, has_side_effects=True, vmem_limit_bytes=40 * 1024 * 1024
+        ),
+        name="prepare",
+    )(part, centroids, growth.reshape(1, cell_rows), weight)
+    tall = 512
+    steps = sites // tall
+    per = tall // LANES
+    whole = lambda shape: pl.BlockSpec(shape, lambda i: (0,) * len(shape))
+    cell_pot, site_pot, barycenter = pl.pallas_call(
+        transport_kernel,
+        grid=(steps,),
+        out_shape=(
+            jax.ShapeDtypeStruct((1, cell_rows), jnp.float32),
+            jax.ShapeDtypeStruct((steps, per, LANES), jnp.float32),
+            jax.ShapeDtypeStruct((sites, features), jnp.float32),
+        ),
+        in_specs=[
+            pl.BlockSpec((tall, features), lambda i: (i, 0)),
+            whole((cells, features)),
+            whole((1, cells)),
+            whole((1, cell_rows)),
+            pl.BlockSpec((1, per, LANES), lambda i: (i, 0, 0)),
+            whole((1, LANES)),
+        ],
+        out_specs=(
+            whole((1, cell_rows)),
+            pl.BlockSpec((1, per, LANES), lambda i: (i, 0, 0)),
+            pl.BlockSpec((tall, features), lambda i: (i, 0)),
+        ),
+        compiler_params=pltpu.CompilerParams(vmem_limit_bytes=40 * 1024 * 1024),
+        name="transport",
+    )(centroids, proj, pot, cell_pot, weight.reshape(steps, per, LANES), total)
+    return cell_pot.reshape(cell_rows), site_pot.reshape(sites), barycenter
+
+
 def solution(mesh):
     placed = (P("cell", "gene"), P("gene", None), P("site", None), P("cell"), P("site"))
+    sizes = dict(mesh.shape)
+    small = sizes["gene"] == 4 and sizes["cell"] == 2 and sizes["site"] == 4
     return jax.shard_map(
-        shards,
+        fused_shards if small else shards,
         mesh=mesh,
         in_specs=placed,
         out_specs=(P("cell"), P("site"), P("site", None)),

time: 256 us -> 58.6 us (0.23)
  waiting for transfers between devices: 107 us -> 0 us
  blocking collectives: 95.9 us -> 0 us
  Pallas kernels: 0 us -> 53.9 us
  other arithmetic: 22.9 us -> 0 us
  between operations: 14.2 us -> 0.7 us
  matrix products: 13.1 us -> 3.89 us
    psum x1 -> x0, waiting for transfers between devices: 107 us -> none  [shards(): summed = lax.psum(carried, 'cell')]
    psum x3 -> x0, blocking collectives: 57.7 us -> none  [the longest x1 45.8 us: shards(): projected = lax.psum(partial_term, 'gene').astype(jnp.bfloat16)]
    pallas_call x0 -> x2, Pallas kernels: none -> 53.9 us  [the longest x1 39.6 us: fused_shards(): pl.pallas_call(prepare_kernel, out_shape=(jax.ShapeDtypeStruct((cells, fe...]
    all_gather x8 -> x0, blocking collectives: 38.2 us -> none  [merged(): gathered = jax.tree.map(lambda a: lax.all_gather(a, axis), part)]
    dot_general x3 -> x1, matrix products: 13.1 us -> 3.89 us  [fused_shards(): part = jnp.dot(quarter, proj_weight, preferred_element_type=jnp.float32)]
    reduce_max x3 -> x0, other arithmetic: 8.64 us -> none  [the longest x2 5.95 us: over_cells(): local_peak = jnp.max(scores, axis=0)]
    reduce_sum x8 -> x0, other arithmetic: 7.19 us -> none  [the longest x1 2.07 us: shards(): cent_norm = jnp.sum(cent_f * cent_f, axis=1) / features]
    div x3 -> x0, other arithmetic: 4.56 us -> none  [the longest x1 4.55 us: shards(): barycenter = summed / site_share[:, None]]
  transfers between devices with their start and end apart: 1 -> 0, of which waited for: 1 -> 0; matrix products, arithmetic and copies ran while one was open for 0% -> 0% of each run, Pallas kernels for 0% -> 0%
where the time goes in v1:
time: 58.6 us; the launch traced here: 58.5 us
  Pallas kernels  53.9 us (92%)
  matrix products  3.89 us (7%)
  between operations  0.7 us (1%)
    pallas_call x1, Pallas kernels, fused_shards(): pl.pallas_call(prepare_kernel, out_shape=(jax.ShapeDtypeStruct((cells, fe...  39.6 us
    pallas_call x1, Pallas kernels, fused_shards(): pl.pallas_call(transport_kernel, grid=(steps,), out_shape=(jax.ShapeDtype...  14.3 us
    dot_general x1, matrix products, fused_shards(): part = jnp.dot(quarter, proj_weight, preferred_element_type=jnp.float32)  3.89 us

profile of v1, /device:TPU:0, one launch (start us, length us, event | category | flops | bytes accessed | tf_op | source)
XLA Modules:
  0.0 58.5 jit_solution(5050117096412096584)
XLA Ops:
  0.6 0.0 copy-start.1
  0.6 0.0 copy-start
  0.7 0.0 copy-start.2
  0.7 3.9 %fusion.part_ref = f32[128,512]{1,0:T(8,128)S(1)} fusion(bf16[5000,512]{1,0:T(8,128)(2,1)} %param.6, bf16[512,5000]{0,1:T(8,128)(2,1)} %param.5, s32[]{:T(128)S(6)} %select_n.3), kind=kOutput, calls=%fused_computation | convolution fusion | flops 655360000 | bytes 6662148 | tf_op jit(solution)/shard_map/dot_general | solution.py:367
  4.6 0.0 copy-done.1
  4.6 0.0 copy-done
  4.6 0.0 copy-done.2
  4.6 39.6 %prepare.1 = (bf16[1024,512]{1,0:T(8,128)(2,1)S(1)}, f32[1,1024]{1,0:T(1,128)S(1)}, f32[1,512]{1,0:T(1,128)S(1)}, f32[1,128]{1,0:T(1,128)S(1)}) custom-call(f32[128,512]{1,0:T(8,128)S(1)} %fusion.part_ref, bf16[2048,512]{1,0:T(8,128)(2,1)S(1)} %copy-done, f32[1,512]{1,0:T(1,128)S(1)} %bitcast.8, f32[16,128]{1,0:T(8,128)S(1)} %bitcast.6), custom_call_target="tpu_custom_call" | custom-call | tf_op jit(solution)/shard_map/prepare/pallas_call | solution.py:371
  44.2 14.3 %transport.1 = (f32[1,512]{1,0:T(1,128)}, f32[4,4,128]{2,1,0:T(4,128)}, f32[2048,512]{1,0:T(8,128)}) custom-call(bf16[2048,512]{1,0:T(8,128)(2,1)S(1)} %copy-done, bf16[1024,512]{1,0:T(8,128)(2,1)S(1)} %get-tuple-element.10.proj_ref, f32[1,1024]{1,0:T(1,128)S(1)} %get-tuple-element.11.pot_ref, f32[1,512]{1,0:T(1,128)S(1)} %get-tuple-element.12.cell_ref, ...), custom_call_target="tpu_custom_call" | custom-call | tf_op jit(solution)/shard_map/transport/pallas_call | solution.py:403
Async XLA Ops:
  0.6 3.9 %copy-start.1 = (f32[2048]{0:T(1024)S(1)}, f32[2048]{0:T(1024)}, u32[]{:S(2)}) copy-start(f32[2048]{0:T(1024)} %param.9) | copy-start | bytes 24580
  0.6 3.9 %copy-start = (bf16[2048,512]{1,0:T(8,128)(2,1)S(1)}, bf16[2048,512]{1,0:T(8,128)(2,1)}, u32[]{:S(2)}) copy-start(bf16[2048,512]{1,0:T(8,128)(2,1)} %cent_ref.1) | copy-start | bytes 6291460
  0.7 3.9 %copy-start.2 = (f32[512]{0:T(512)S(1)}, f32[512]{0:T(512)}, u32[]{:S(2)}) copy-start(f32[512]{0:T(512)} %param.8) | copy-start | bytes 6148

commit v2 on v1

--- a/solution.py
+++ b/solution.py
@@ -113,9 +113,9 @@
     return jnp.broadcast_to(total, (block.shape[0], LANES))
 
 
-def fold(scores_ref, pot, start, lane, state):
+def fold(scores_ref, pot, start, lane_start, state):
     peak, total = state
-    block = scores_ref[pl.ds(start, TALL), lane * LANES : (lane + 1) * LANES]
+    block = scores_ref[pl.ds(start, TALL), pl.ds(lane_start, LANES)]
     block = (block + pot).reshape(TALL // 8, 8, LANES)
     new_peak = jnp.maximum(peak, jnp.max(block, axis=0))
     total = total * jnp.exp2(peak - new_peak) + jnp.sum(jnp.exp2(block - new_peak[None]), axis=0)
@@ -130,8 +130,8 @@
 
 def prepare_kernel(
     part_ref, cent_hbm, growth_ref, weight_ref,
-    proj_out, pot_out, cell_out, weight_out,
-    cent, arrived, proj, scores, site_pot, log_share, grow, message,
+    proj_out, pot_out, cell_out, weight_out, scores, weight_col, norm_out,
+    cent, arrived, proj, site_pot, grow, message,
     local_sem, reduce_send, reduce_recv, z_send, z_recv, x_send, x_recv, y_send, y_recv,
     diag_send, diag_recv, core_send, core_recv, grow_send, grow_recv, lse_send, lse_recv,
 ):
@@ -186,8 +186,10 @@
 
     def norms(step, carry):
         start = pl.multiple_of(step * LANES, LANES)
-        site_pot[pl.ds(start, LANES), :] = -scaled_norms(cent[pl.ds(start, LANES), :], norm_scale)
-        log_share[pl.ds(start, LANES), :] = to_column(weight_ref[pl.ds(step, 1), :])
+        norm = scaled_norms(cent[pl.ds(start, LANES), :], norm_scale)
+        site_pot[pl.ds(start, LANES), :] = -norm
+        norm_out[pl.ds(step, 1), :] = to_row(norm)
+        weight_col[pl.ds(start, LANES), :] = to_column(weight_ref[pl.ds(step, 1), :])
         return carry
 
     lax.fori_loop(0, sites // LANES, norms, 0)
@@ -237,33 +239,52 @@
             send(block, diag_send.at[d], diag_recv.at[d], x_dev)
     send(group(cell, x_site), core_send.at[1], core_recv.at[1], core_dev)
     send(group(other_cell, site), core_send.at[2], core_recv.at[2], core_dev)
+    scale = 2.0 * norm_scale
+    blocks = cells // LANES
+    half_blocks = cell_rows // LANES
+    bulk = 1024
+    start_state = (
+        jnp.full((8, LANES), -1e38, jnp.float32), jnp.zeros((8, LANES), jnp.float32)
+    )
+
+    def await_groups(pairs):
+        for at, cell_at, site_at in pairs:
+            await_piece(group(cell_at, site_at), core_send.at[at], core_recv.at[at], core_dev)
+
+    def first(cell_at, start, states):
+        side = pl.multiple_of(cell_at * cell_rows, cell_rows)
+        scores[start : start + bulk, pl.ds(side, cell_rows)] = scale * lax.dot_general(
+            cent[start : start + bulk, :], proj[pl.ds(side, cell_rows), :],
+            (((1,), (1,)), ((), ())), preferred_element_type=jnp.float32,
+        )
+
+        def add(step, states):
+            at = pl.multiple_of(start + step * TALL, TALL)
+            pot = site_pot[pl.ds(at, TALL), :]
+            return tuple(
+                fold(scores, pot, at, pl.multiple_of(side + lane * LANES, LANES), states[lane])
+                for lane in range(half_blocks)
+            )
+
+        return lax.fori_loop(0, bulk // TALL, add, states)
+
+    await_groups(((0, cell, core_site), (1, cell, far_site)))
+    here = first(cell, 0, (start_state,) * half_blocks)
     for d in range(GENE):
         await_piece(
             rows(other_cell, x_site, back[d]), diag_send.at[d], diag_recv.at[d],
             y_dev if d < 2 else x_dev,
         )
     send(group(other_cell, x_site), core_send.at[3], core_recv.at[3], core_dev)
-    for at, (cell_at, site_at) in enumerate(
-        ((cell, core_site), (cell, far_site), (other_cell, core_site), (other_cell, far_site))
-    ):
-        await_piece(group(cell_at, site_at), core_send.at[at], core_recv.at[at], core_dev)
-
-    scale = 2.0 * norm_scale
-    blocks = cells // LANES
-    start_state = (
-        jnp.full((8, LANES), -1e38, jnp.float32), jnp.zeros((8, LANES), jnp.float32)
-    )
-
-    def first(step, states):
-        start = pl.multiple_of(step * TALL, TALL)
-        scores[pl.ds(start, TALL), :] = scale * lax.dot_general(
-            cent[pl.ds(start, TALL), :], proj[...], (((1,), (1,)), ((), ())),
-            preferred_element_type=jnp.float32,
-        )
-        pot = site_pot[pl.ds(start, TALL), :]
-        return tuple(fold(scores, pot, start, lane, states[lane]) for lane in range(blocks))
-
-    states = lax.fori_loop(0, sites // TALL, first, (start_state,) * blocks)
+    for start in range(bulk, sites, bulk):
+        here = first(cell, start, here)
+    await_groups(((2, other_cell, core_site), (3, other_cell, far_site)))
+    there = (start_state,) * half_blocks
+    for start in range(0, sites, bulk):
+        there = first(other_cell, start, there)
+    is_low = cell == 0
+    pick = functools.partial(jax.tree.map, lambda p, q: jnp.where(is_low, p, q))
+    states = pick(here, there) + pick(there, here)
 
     def exchange(turn, states):
         closed = [close(state) for state in states]
@@ -299,10 +320,10 @@
             block = scores[at, :] + pot
             peak = jnp.max(block, axis=1, keepdims=True)
             summed = jnp.sum(jnp.exp2(block - peak), axis=1, keepdims=True)
-            share = log_share[at, :] / weight_total
+            share = weight_col[at, :] / weight_total
             site_pot[at, :] = jnp.log(share / summed) * LOG2E - peak
         new = site_pot[pl.ds(start, TALL), :]
-        return tuple(fold(scores, new, start, lane, states[lane]) for lane in range(blocks))
+        return tuple(fold(scores, new, start, lane * LANES, states[lane]) for lane in range(blocks))
 
     states = lax.fori_loop(0, sites // TALL, second, (start_state,) * blocks)
     lse, _ = exchange(1, states)
@@ -329,33 +350,52 @@
 
 
 def transport_kernel(
-    cent_ref, proj_ref, pot_ref, cell_ref, weight_ref, total_ref, cell_out, site_out, bary_out
+    scores, proj, pot_ref, cell_ref, weight_col, total_ref, norm_ref,
+    cell_out, site_out, bary_hbm, coupling, bary, sems,
 ):
-    features = cent_ref.shape[1]
-    norm_scale = LOG2E / (features * EPSILON)
+    sites, features = bary.shape
+    cells = scores.shape[1]
+    rows_at_once = 32
     cell_out[...] = cell_ref[...]
     pot = pot_ref[...]
     weight_total = total_ref[...]
-    count = cent_ref.shape[0] // LANES
-    for sub in range(count):
-        at = pl.ds(sub * LANES, LANES)
-        cent = cent_ref[at, :]
-        block = (2.0 * norm_scale) * lax.dot_general(
-            cent, proj_ref[...], (((1,), (1,)), ((), ())), preferred_element_type=jnp.float32
-        )
-        block = block + pot
-        peak = jnp.max(block, axis=1, keepdims=True)
-        block = jnp.exp2(block - peak)
-        summed = jnp.sum(block, axis=1, keepdims=True)
-        share = to_column(weight_ref[0, sub : sub + 1, :]) / weight_total
-        ratio = share / summed
-        site_pot = (EPSILON * LN2) * (jnp.log(ratio) * LOG2E - peak) + scaled_norms(
-            cent, 1.0 / features
-        )
-        site_out[0, sub : sub + 1, :] = to_row(site_pot)
-        coupling = (block * tiled(ratio, block.shape[1])).astype(jnp.bfloat16)
-        carried = jnp.dot(coupling, proj_ref[...], preferred_element_type=jnp.float32)
-        bary_out[at, :] = carried * tiled(1.0 / share, features)
+
+    def couple(chunk):
+        slot = chunk % 2
+        for base in range(0, TALL, LANES):
+            columns = []
+            for sub in range(base, base + LANES, rows_at_once):
+                at = pl.ds(chunk * TALL + sub, rows_at_once)
+                block = scores[at, :] + pot
+                peak = jnp.max(block, axis=1, keepdims=True)
+                block = jnp.exp2(block - peak)
+                summed = jnp.sum(block, axis=1, keepdims=True)
+                ratio = weight_col[at, :] / weight_total / summed
+                columns.append(jnp.log(ratio) * LOG2E - peak)
+                coupling[slot, sub : sub + rows_at_once, :] = (
+                    block * tiled(ratio, cells)
+                ).astype(jnp.bfloat16)
+            row = (chunk * TALL + base) // LANES
+            pot_row = to_row(jnp.concatenate(columns, axis=0))
+            site_out[row : row + 1, :] = (EPSILON * LN2) * (pot_row + norm_ref[row : row + 1, :])
+
+    def carry(chunk):
+        at = pl.ds(chunk * TALL, TALL)
+        carried = jnp.dot(coupling[chunk % 2], proj[...], preferred_element_type=jnp.float32)
+        bary[at, :] = carried * tiled(weight_total / weight_col[at, :], features)
+        copy = pltpu.make_async_copy(bary.at[at], bary_hbm.at[at], sems.at[chunk])
+        copy.start()
+        return copy
+
+    copies = []
+    chunks = sites // TALL
+    couple(0)
+    for chunk in range(chunks):
+        if chunk + 1 < chunks:
+            couple(chunk + 1)
+        copies.append(carry(chunk))
+    for copy in copies:
+        copy.wait()
 
 
 def fused_shards(expr, proj_weight, centroids, growth, site_weight):
@@ -368,22 +408,23 @@
     vmem = pl.BlockSpec(memory_space=pltpu.VMEM)
     weight = site_weight.reshape(sites // LANES, LANES)
     dma = pltpu.SemaphoreType.DMA
-    proj, pot, cell_pot, total = pl.pallas_call(
+    proj, pot, cell_pot, total, scores, weight_col, norm = pl.pallas_call(
         prepare_kernel,
         out_shape=(
             jax.ShapeDtypeStruct((cells, features), jnp.bfloat16),
             jax.ShapeDtypeStruct((1, cells), jnp.float32),
             jax.ShapeDtypeStruct((1, cell_rows), jnp.float32),
             jax.ShapeDtypeStruct((1, LANES), jnp.float32),
+            jax.ShapeDtypeStruct((sites, cells), jnp.float32),
+            jax.ShapeDtypeStruct((sites, LANES), jnp.float32),
+            jax.ShapeDtypeStruct((sites // LANES, LANES), jnp.float32),
         ),
         in_specs=[vmem, pl.BlockSpec(memory_space=pl.ANY), vmem, vmem],
-        out_specs=(vmem,) * 4,
+        out_specs=(vmem,) * 7,
         scratch_shapes=[
             pltpu.VMEM((sites, features), jnp.bfloat16),
             pltpu.VMEM((GENE - 1, strip // GENE, features), jnp.float32),
             pltpu.VMEM((cells, features), jnp.bfloat16),
-            pltpu.VMEM((sites, cells), jnp.float32),
-            pltpu.VMEM((sites, LANES), jnp.float32),
             pltpu.VMEM((sites, LANES), jnp.float32),
             pltpu.VMEM((CELL, 1, cell_rows), jnp.float32),
             pltpu.VMEM((ROUNDS, SITE, 1, 2 * cells + LANES), jnp.float32),
@@ -392,38 +433,27 @@
             dma, dma, dma((ROUNDS, 3)), dma((ROUNDS, 3)),
         ],
         compiler_params=pltpu.CompilerParams(
-            collective_id=0, has_side_effects=True, vmem_limit_bytes=40 * 1024 * 1024
+            collective_id=0, has_side_effects=True, vmem_limit_bytes=36 * 1024 * 1024
         ),
         name="prepare",
     )(part, centroids, growth.reshape(1, cell_rows), weight)
-    tall = 512
-    steps = sites // tall
-    per = tall // LANES
-    whole = lambda shape: pl.BlockSpec(shape, lambda i: (0,) * len(shape))
     cell_pot, site_pot, barycenter = pl.pallas_call(
         transport_kernel,
-        grid=(steps,),
         out_shape=(
             jax.ShapeDtypeStruct((1, cell_rows), jnp.float32),
-            jax.ShapeDtypeStruct((steps, per, LANES), jnp.float32),
+            jax.ShapeDtypeStruct((sites // LANES, LANES), jnp.float32),
             jax.ShapeDtypeStruct((sites, features), jnp.float32),
         ),
-        in_specs=[
-            pl.BlockSpec((tall, features), lambda i: (i, 0)),
-            whole((cells, features)),
-            whole((1, cells)),
-            whole((1, cell_rows)),
-            pl.BlockSpec((1, per, LANES), lambda i: (i, 0, 0)),
-            whole((1, LANES)),
+        in_specs=[vmem] * 7,
+        out_specs=(vmem, vmem, pl.BlockSpec(memory_space=pl.ANY)),
+        scratch_shapes=[
+            pltpu.VMEM((2, TALL, cells), jnp.bfloat16),
+            pltpu.VMEM((sites, features), jnp.float32),
+            dma((sites // TALL,)),
         ],
-        out_specs=(
-            whole((1, cell_rows)),
-            pl.BlockSpec((1, per, LANES), lambda i: (i, 0, 0)),
-            pl.BlockSpec((tall, features), lambda i: (i, 0)),
-        ),
-        compiler_params=pltpu.CompilerParams(vmem_limit_bytes=40 * 1024 * 1024),
+        compiler_params=pltpu.CompilerParams(vmem_limit_bytes=36 * 1024 * 1024),
         name="transport",
-    )(centroids, proj, pot, cell_pot, weight.reshape(steps, per, LANES), total)
+    )(scores, proj, pot, cell_pot, weight_col, total, norm)
     return cell_pot.reshape(cell_rows), site_pot.reshape(sites), barycenter
 
 

time: 58.6 us -> 47.9 us (0.82)
  Pallas kernels: 53.9 us -> 43.1 us
    pallas_call x1, Pallas kernels: 14.3 us -> 4.74 us  [fused_shards(): pl.pallas_call(transport_kernel, out_shape=(jax.ShapeDtypeStruct((1, cell...]
    pallas_call x1, Pallas kernels: 39.6 us -> 38.4 us  [fused_shards(): pl.pallas_call(prepare_kernel, out_shape=(jax.ShapeDtypeStruct((cells, fe...]
where the time goes in v2:
time: 47.9 us; the launch traced here: 47.7 us
  Pallas kernels  43.1 us (90%)
  matrix products  3.89 us (8%)
  between operations  0.7 us (1%)
    pallas_call x1, Pallas kernels, fused_shards(): pl.pallas_call(prepare_kernel, out_shape=(jax.ShapeDtypeStruct((cells, fe...  38.4 us
    pallas_call x1, Pallas kernels, fused_shards(): pl.pallas_call(transport_kernel, out_shape=(jax.ShapeDtypeStruct((1, cell...  4.74 us
    dot_general x1, matrix products, fused_shards(): part = jnp.dot(quarter, proj_weight, preferred_element_type=jnp.float32)  3.89 us

profile of v2, /device:TPU:0, one launch (start us, length us, event | category | flops | bytes accessed | tf_op | source)
XLA Modules:
  0.0 47.7 jit_solution(10188481149156423492)
XLA Ops:
  0.6 0.0 copy-start.1
  0.6 0.0 copy-start.2
  0.7 0.0 copy-start
  0.7 3.9 %fusion.part_ref = f32[128,512]{1,0:T(8,128)S(1)} fusion(bf16[5000,512]{1,0:T(8,128)(2,1)} %param.6, bf16[512,5000]{0,1:T(8,128)(2,1)} %param.5, s32[]{:T(128)S(6)} %select_n.3), kind=kOutput, calls=%fused_computation | convolution fusion | flops 655360000 | bytes 6662148 | tf_op jit(solution)/shard_map/dot_general | solution.py:407
  4.6 0.0 copy-done.1
  4.6 0.0 copy-done.2
  4.6 0.0 copy-done
  4.6 38.4 %prepare.1 = (bf16[1024,512]{1,0:T(8,128)(2,1)S(1)}, f32[1,1024]{1,0:T(1,128)S(1)}, f32[1,512]{1,0:T(1,128)S(1)}, f32[1,128]{1,0:T(1,128)S(1)}, f32[2048,1024]{1...) custom-call(f32[128,512]{1,0:T(8,128)S(1)} %fusion.part_ref, bf16[2048,512]{1,0:T(8,128)(2,1)S(1)} %copy-done, ...), custom_call_target="tpu_custom_call" | custom-call | tf_op jit(solution)/shard_map/prepare/pallas_call | solution.py:411
  43.0 4.7 %transport.1 = (f32[1,512]{1,0:T(1,128)}, f32[16,128]{1,0:T(8,128)}, f32[2048,512]{1,0:T(8,128)}) custom-call(f32[2048,1024]{1,0:T(8,128)S(1)} %get-tuple-element.13.scores, bf16[1024,512]{1,0:T(8,128)(2,1)S(1)} %get-tuple-element.14.proj, f32[1,1024]{1,0:T(1,128)S(1)} %get-tuple-element.15.pot_ref, f32[1,512]{1,0:T(1,128)S(1)} %get-tuple-element.16.cell_ref, ...), custom_call_target="tpu_custom_call" | custom-call | tf_op jit(solution)/shard_map/transport/pallas_call | solution.py:440
Async XLA Ops:
  0.6 3.9 %copy-start.1 = (f32[2048]{0:T(1024)S(1)}, f32[2048]{0:T(1024)}, u32[]{:S(2)}) copy-start(f32[2048]{0:T(1024)} %param.9) | copy-start | bytes 24580
  0.6 3.9 %copy-start.2 = (f32[512]{0:T(512)S(1)}, f32[512]{0:T(512)}, u32[]{:S(2)}) copy-start(f32[512]{0:T(512)} %param.8) | copy-start | bytes 6148
  0.7 3.9 %copy-start = (bf16[2048,512]{1,0:T(8,128)(2,1)S(1)}, bf16[2048,512]{1,0:T(8,128)(2,1)}, u32[]{:S(2)}) copy-start(bf16[2048,512]{1,0:T(8,128)(2,1)} %cent_hbm.1) | copy-start | bytes 6291460

commit v3 on v2

--- a/solution.py
+++ b/solution.py
@@ -242,7 +242,7 @@
     scale = 2.0 * norm_scale
     blocks = cells // LANES
     half_blocks = cell_rows // LANES
-    bulk = 1024
+    bulk = 512
     start_state = (
         jnp.full((8, LANES), -1e38, jnp.float32), jnp.zeros((8, LANES), jnp.float32)
     )
@@ -251,37 +251,46 @@
         for at, cell_at, site_at in pairs:
             await_piece(group(cell_at, site_at), core_send.at[at], core_recv.at[at], core_dev)
 
-    def first(cell_at, start, states):
+    def score(cell_at, start):
         side = pl.multiple_of(cell_at * cell_rows, cell_rows)
         scores[start : start + bulk, pl.ds(side, cell_rows)] = scale * lax.dot_general(
             cent[start : start + bulk, :], proj[pl.ds(side, cell_rows), :],
             (((1,), (1,)), ((), ())), preferred_element_type=jnp.float32,
         )
 
-        def add(step, states):
-            at = pl.multiple_of(start + step * TALL, TALL)
-            pot = site_pot[pl.ds(at, TALL), :]
-            return tuple(
+    def add(cell_at, start, states):
+        side = pl.multiple_of(cell_at * cell_rows, cell_rows)
+        for at in range(start, start + bulk, TALL):
+            pot = site_pot[at : at + TALL, :]
+            states = tuple(
                 fold(scores, pot, at, pl.multiple_of(side + lane * LANES, LANES), states[lane])
                 for lane in range(half_blocks)
             )
-
-        return lax.fori_loop(0, bulk // TALL, add, states)
+        return states
 
     await_groups(((0, cell, core_site), (1, cell, far_site)))
-    here = first(cell, 0, (start_state,) * half_blocks)
+    here = there = (start_state,) * half_blocks
+    middle = sites // 2
+    score(cell, 0)
+    for start in range(bulk, middle, bulk):
+        here = add(cell, start - bulk, here)
+        score(cell, start)
     for d in range(GENE):
         await_piece(
             rows(other_cell, x_site, back[d]), diag_send.at[d], diag_recv.at[d],
             y_dev if d < 2 else x_dev,
         )
     send(group(other_cell, x_site), core_send.at[3], core_recv.at[3], core_dev)
+    for start in range(middle, sites, bulk):
+        here = add(cell, start - bulk, here)
+        score(cell, start)
+    await_groups(((2, other_cell, core_site), (3, other_cell, far_site)))
+    here = add(cell, sites - bulk, here)
+    score(other_cell, 0)
     for start in range(bulk, sites, bulk):
-        here = first(cell, start, here)
-    await_groups(((2, other_cell, core_site), (3, other_cell, far_site)))
-    there = (start_state,) * half_blocks
-    for start in range(0, sites, bulk):
-        there = first(other_cell, start, there)
+        there = add(other_cell, start - bulk, there)
+        score(other_cell, start)
+    there = add(other_cell, sites - bulk, there)
     is_low = cell == 0
     pick = functools.partial(jax.tree.map, lambda p, q: jnp.where(is_low, p, q))
     states = pick(here, there) + pick(there, here)
@@ -313,8 +322,7 @@
 
     rows_at_once = 32
 
-    def second(step, states):
-        start = pl.multiple_of(step * TALL, TALL)
+    def repot(start):
         for sub in range(TALL // rows_at_once):
             at = pl.ds(start + sub * rows_at_once, rows_at_once)
             block = scores[at, :] + pot
@@ -322,10 +330,21 @@
             summed = jnp.sum(jnp.exp2(block - peak), axis=1, keepdims=True)
             share = weight_col[at, :] / weight_total
             site_pot[at, :] = jnp.log(share / summed) * LOG2E - peak
+
+    def refold(start, states):
         new = site_pot[pl.ds(start, TALL), :]
-        return tuple(fold(scores, new, start, lane * LANES, states[lane]) for lane in range(blocks))
-
-    states = lax.fori_loop(0, sites // TALL, second, (start_state,) * blocks)
+        return tuple(
+            fold(scores, new, start, lane * LANES, states[lane]) for lane in range(blocks)
+        )
+
+    def second(step, states):
+        states = refold(pl.multiple_of((step - 1) * TALL, TALL), states)
+        repot(pl.multiple_of(step * TALL, TALL))
+        return states
+
+    repot(0)
+    states = lax.fori_loop(1, sites // TALL, second, (start_state,) * blocks)
+    states = refold(sites - TALL, states)
     lse, _ = exchange(1, states)
     pot = log_a - lse
 

time: 47.9 us -> 47.9 us (level)
  no operation moved by 1% of the time
where the time goes in v3:
time: 47.9 us; the launch traced here: 47.7 us
  Pallas kernels  43.1 us (90%)
  matrix products  3.89 us (8%)
  between operations  0.7 us (1%)
    pallas_call x1, Pallas kernels, fused_shards(): pl.pallas_call(prepare_kernel, out_shape=(jax.ShapeDtypeStruct((cells, fe...  38.4 us
    pallas_call x1, Pallas kernels, fused_shards(): pl.pallas_call(transport_kernel, out_shape=(jax.ShapeDtypeStruct((1, cell...  4.74 us
    dot_general x1, matrix products, fused_shards(): part = jnp.dot(quarter, proj_weight, preferred_element_type=jnp.float32)  3.89 us

profile of v3, /device:TPU:0, one launch (start us, length us, event | category | flops | bytes accessed | tf_op | source)
XLA Modules:
  0.0 47.7 jit_solution(9600364525050101966)
XLA Ops:
  0.6 0.0 copy-start.1
  0.6 0.0 copy-start.2
  0.7 0.0 copy-start
  0.7 3.9 %fusion.part_ref = f32[128,512]{1,0:T(8,128)S(1)} fusion(bf16[5000,512]{1,0:T(8,128)(2,1)} %param.6, bf16[512,5000]{0,1:T(8,128)(2,1)} %param.5, s32[]{:T(128)S(6)} %select_n.3), kind=kOutput, calls=%fused_computation | convolution fusion | flops 655360000 | bytes 6662148 | tf_op jit(solution)/shard_map/dot_general | solution.py:426
  4.6 0.0 copy-done.1
  4.6 0.0 copy-done.2
  4.6 0.0 copy-done
  4.6 38.4 %prepare.1 = (bf16[1024,512]{1,0:T(8,128)(2,1)S(1)}, f32[1,1024]{1,0:T(1,128)S(1)}, f32[1,512]{1,0:T(1,128)S(1)}, f32[1,128]{1,0:T(1,128)S(1)}, f32[2048,1024]{1...) custom-call(f32[128,512]{1,0:T(8,128)S(1)} %fusion.part_ref, bf16[2048,512]{1,0:T(8,128)(2,1)S(1)} %copy-done, ...), custom_call_target="tpu_custom_call" | custom-call | tf_op jit(solution)/shard_map/prepare/pallas_call | solution.py:430
  43.0 4.7 %transport.1 = (f32[1,512]{1,0:T(1,128)}, f32[16,128]{1,0:T(8,128)}, f32[2048,512]{1,0:T(8,128)}) custom-call(f32[2048,1024]{1,0:T(8,128)S(1)} %get-tuple-element.13.scores, bf16[1024,512]{1,0:T(8,128)(2,1)S(1)} %get-tuple-element.14.proj, f32[1,1024]{1,0:T(1,128)S(1)} %get-tuple-element.15.pot_ref, f32[1,512]{1,0:T(1,128)S(1)} %get-tuple-element.16.cell_ref, ...), custom_call_target="tpu_custom_call" | custom-call | tf_op jit(solution)/shard_map/transport/pallas_call | solution.py:459
Async XLA Ops:
  0.6 3.9 %copy-start.1 = (f32[2048]{0:T(1024)S(1)}, f32[2048]{0:T(1024)}, u32[]{:S(2)}) copy-start(f32[2048]{0:T(1024)} %param.9) | copy-start | bytes 24580
  0.6 3.9 %copy-start.2 = (f32[512]{0:T(512)S(1)}, f32[512]{0:T(512)}, u32[]{:S(2)}) copy-start(f32[512]{0:T(512)} %param.8) | copy-start | bytes 6148
  0.7 3.9 %copy-start = (bf16[2048,512]{1,0:T(8,128)(2,1)S(1)}, bf16[2048,512]{1,0:T(8,128)(2,1)}, u32[]{:S(2)}) copy-start(bf16[2048,512]{1,0:T(8,128)(2,1)} %cent_hbm.1) | copy-start | bytes 6291460
